TPU v7x, 32 devices: a whole 2x2x4 slice. The times are simulated.
32 devices in a mesh: tm: 8 (over y, x, core), batch: 4 (over z).
Axes of the slice: x: 2, y: 2, z: 4, core: 2. Of those that a mesh axis runs over, the one named last changes fastest.
Arguments:
- signal: bfloat16 [4, 1024, 4096], P('batch', 'tm'), may hold values from -7.5 to 7.5
- gate_input: bfloat16 [4, 1024, 4096], P('batch', 'tm'), may hold values from -6 to 6
- bc_forward: bfloat16 [4, 1024, 128], P('batch', 'tm'), may hold values from -6 to 6
- bc_backward: bfloat16 [4, 1024, 128], P('batch', 'tm'), may hold values from -6 to 6
- step_raw: bfloat16 [4, 1024, 128], P('batch', 'tm'), may hold values from -12 to 2
- decay_rate: float32 [2, 64], replicated, may hold values from 0.3 to 1
- conv_weight: float32 [2, 4, 4224], replicated, may hold values from -3 to 3
- conv_bias: float32 [2, 4224], replicated, may hold values from -1.5 to 1.5
- skip_gain: float32 [2, 64], replicated, may hold values from 0.5 to 1.5
- norm_gain: float32 [4096], replicated, may hold values from 0.1 to 1.9
Outputs:
- mixed: bfloat16 [4, 1024, 4096], P(None, 'batch', 'tm')
All inputs are finite; a program needn't handle non-finite values.
Results may differ from a plain program's by a relative error of at most 0.0075.
Values may be sent and summed in bfloat16 or wider, within the bound.
A program may use at most 256 MiB of HBM per device.

v0:
```python
import jax
import jax.numpy as jnp
from jax import lax
from jax.sharding import PartitionSpec as P

INNER = 4096
HEADDIM = 64
STATE = 64
GROUP = 128
HEADS = 64


EPSILON = 1e-05


def from_behind(array, axis, by):
    devices = lax.axis_size(axis)
    pairs = [(i, i + by) for i in range(devices) if 0 <= i + by < devices]
    return lax.ppermute(array, axis, pairs)


def entering(value, axis, join, neutral):
    count, mine = (lax.axis_size(axis), lax.axis_index(axis))
    pieces = jax.tree.map(lambda part: lax.all_gather(part, axis), value)
    running = jax.tree.map(
        lambda part, zero: jnp.full_like(part, 0) + jnp.asarray(zero, part.dtype), value, neutral
    )

    def lap(position, running):
        longer = join(running, jax.tree.map(lambda part: part[position], pieces))
        return jax.tree.map(lambda new, old: jnp.where(position < mine, new, old), longer, running)

    return lax.fori_loop(0, count - 1, lap, running)


def carried_in(array, axis, join, neutral):
    count = lax.axis_size(axis)
    place = lax.axis_index(axis)
    ahead = count - 1 - place
    gathered = jax.tree.map(
        lambda a, kind: lax.all_gather(a.astype(kind), axis), array, (jnp.bfloat16, jnp.bfloat16)
    )
    state = jax.tree.map(lambda a, e: jnp.zeros_like(a) + jnp.asarray(e, a.dtype), array, neutral)

    def one(lap, state):
        source = count - 1 - lap
        return join(
            state,
            jax.tree.map(
                lambda a, own: lax.dynamic_index_in_dim(a, source, 0, False).astype(own.dtype),
                gathered,
                array,
            ),
        )

    return lax.fori_loop(0, ahead, one, state)


def conv_silu(sequence, history, weights, offsets):
    length = sequence.shape[0]
    padded = jnp.concatenate([history, sequence], 0).astype(jnp.float32)
    combined_waveform = jnp.broadcast_to(offsets[None, :], (length, sequence.shape[1]))
    for offset in range(weights.shape[0]):
        combined_waveform = (
            combined_waveform + weights[offset][None, :] * padded[offset : offset + length]
        )
    return jax.nn.silu(combined_waveform).astype(jnp.bfloat16)


def block_parts(x_part, b_part, step_size, rate_head):
    log_decay = -step_size * rate_head[None, None, :]
    cum_log = jnp.cumsum(log_decay, axis=1)
    weight_end = jnp.exp(cum_log[:, -1:, :] - cum_log) * step_size
    b_scaled = (b_part.astype(jnp.float32)[:, :, None, :] * weight_end[..., None]).astype(
        jnp.bfloat16
    )
    states = jnp.einsum("mqhn,mqhp->mhnp", b_scaled, x_part, preferred_element_type=jnp.float32)
    return (cum_log, states, jnp.exp(cum_log[:, -1, :]))


def prepare(x_conv, bc_conv, step_raw, rate_head):
    block_count = x_conv.shape[0] // GROUP
    x_part = x_conv.reshape(block_count, GROUP, -1, HEADDIM)
    b_part = bc_conv[:, :STATE].reshape(block_count, GROUP, STATE)
    c_part = bc_conv[:, STATE:].reshape(block_count, GROUP, STATE)
    step_size = jax.nn.softplus(step_raw.astype(jnp.float32)).reshape(block_count, GROUP, -1)
    cum_log, states, decays = block_parts(x_part, b_part, step_size, rate_head)
    return (x_part, b_part, c_part, step_size, cum_log, states, decays)


def summarize(states, decays):

    def absorb(state_in, pieces):
        return (pieces[1][:, None, None] * state_in + pieces[0], None)

    final_state, _ = lax.scan(absorb, jnp.zeros(states.shape[1:], jnp.float32), (states, decays))
    return (jnp.prod(decays, axis=0), final_state)


def carried_term(c_block, state_in):
    state_high = state_in.astype(jnp.bfloat16)
    state_low = (state_in - state_high.astype(jnp.float32)).astype(jnp.bfloat16)
    upper = jnp.einsum("in,hnp->ihp", c_block, state_high, preferred_element_type=jnp.float32)
    lower = jnp.einsum("in,hnp->ihp", c_block, state_low, preferred_element_type=jnp.float32)
    return upper + lower


def block_outputs(parts, start, skip_head):
    block_len = parts[0].shape[1]
    causal_mask = jnp.arange(block_len)[:, None] >= jnp.arange(block_len)[None, :]

    def advance(state_in, pieces):
        x_block, b_block, c_block, step_block, cum_block, state_block, decay_block = pieces
        scores = jnp.dot(c_block, b_block.T, preferred_element_type=jnp.float32)
        differ = cum_block.T[:, :, None] - cum_block.T[:, None, :]
        masked = jnp.where(causal_mask[None], jnp.exp(jnp.minimum(differ, 0.0)), 0.0)
        mixing = (masked * scores[None] * step_block.T[:, None, :]).astype(jnp.bfloat16)
        local_out = jnp.einsum("hij,jhp->ihp", mixing, x_block, preferred_element_type=jnp.float32)
        carried = carried_term(c_block, state_in)
        result = (
            local_out
            + jnp.exp(cum_block)[:, :, None] * carried
            + skip_head[None, :, None] * x_block.astype(jnp.float32)
        )
        new_state = decay_block[:, None, None] * state_in + state_block
        return (new_state, result.astype(jnp.bfloat16))

    _, outputs = lax.scan(advance, start, parts)
    return outputs.reshape(outputs.shape[0] * outputs.shape[1], -1)


def combine(earlier, later):
    return (earlier[0] * later[0], earlier[1] * later[0][:, None, None] + later[1])


def gated_rows(forward_out, backward_out, gate_rows):
    return (forward_out.astype(jnp.float32) + backward_out.astype(jnp.float32)) * jax.nn.silu(
        gate_rows.astype(jnp.float32)
    )


def shards(
    signal,
    gate_input,
    bc_forward,
    bc_backward,
    step_raw,
    decay_rate,
    conv_weight,
    conv_bias,
    skip_gain,
    norm_gain,
):
    rim_rows = conv_weight.shape[1] - 1
    signal_dev = signal[0]
    bcf_dev = bc_forward[0]
    bcb_dev = bc_backward[0]
    step_dev = step_raw[0]
    left_rim = from_behind(
        jnp.concatenate([signal_dev[-rim_rows:], bcf_dev[-rim_rows:]], 1), "tm", 1
    )
    right_rim = from_behind(
        jnp.concatenate([signal_dev[:rim_rows], bcb_dev[:rim_rows]], 1), "tm", -1
    )
    fwd_parts = prepare(
        conv_silu(signal_dev, left_rim[:, :INNER], conv_weight[0, :, :INNER], conv_bias[0, :INNER]),
        conv_silu(bcf_dev, left_rim[:, INNER:], conv_weight[0, :, INNER:], conv_bias[0, INNER:]),
        step_dev[:, :HEADS],
        decay_rate[0],
    )
    back_history = right_rim[::-1]
    bwd_parts = prepare(
        conv_silu(
            signal_dev[::-1],
            back_history[:, :INNER],
            conv_weight[1, :, :INNER],
            conv_bias[1, :INNER],
        ),
        conv_silu(
            bcb_dev[::-1], back_history[:, INNER:], conv_weight[1, :, INNER:], conv_bias[1, INNER:]
        ),
        step_dev[::-1, HEADS:],
        decay_rate[1],
    )
    fwd_decay, fwd_state = summarize(fwd_parts[5], fwd_parts[6])
    bwd_decay, bwd_state = summarize(bwd_parts[5], bwd_parts[6])
    empty_decay = jnp.ones((HEADS,), jnp.float32)
    empty_state = jnp.zeros((HEADS, STATE, HEADDIM), jnp.float32)
    fwd_in = entering((fwd_decay, fwd_state), "tm", combine, (empty_decay, empty_state))
    bwd_in = carried_in((bwd_decay, bwd_state), "tm", combine, (empty_decay, empty_state))
    forward_out = block_outputs(fwd_parts, fwd_in[1], skip_gain[0])
    backward_out = block_outputs(bwd_parts, bwd_in[1], skip_gain[1])[::-1]
    gated = gated_rows(forward_out, backward_out, gate_input[0])
    inv_rms = lax.rsqrt(jnp.mean(gated * gated, axis=-1, keepdims=True) + EPSILON)
    normed = (gated * inv_rms * norm_gain[None, :]).astype(jnp.bfloat16)
    return lax.all_to_all(
        lax.all_to_all(normed[None], "tm", split_axis=2, concat_axis=1, tiled=True),
        "batch",
        split_axis=1,
        concat_axis=0,
        tiled=True,
    )


def solution(mesh):
    in_specs = (
        P("batch", "tm", None),
        P("batch", "tm", None),
        P("batch", "tm", None),
        P("batch", "tm", None),
        P("batch", "tm", None),
        P(),
        P(),
        P(),
        P(),
        P(),
    )
    out_specs = P(None, "batch", "tm")
    return jax.shard_map(shards, mesh=mesh, in_specs=in_specs, out_specs=out_specs, check_vma=False)
```

profile of v0, /device:TPU:0, one launch (start us, length us, event | category | flops | bytes accessed | tf_op | source)
XLA Modules:
  0.0 313.0 jit_solution(16525662981348647250)
XLA Ops:
  8.2 2.4 collective-permute-start
  12.6 1.9 fusion.75
  14.5 1.5 slice_bitcast_fusion.8
  19.8 1.5 fusion.76
  21.4 1.3 slice_bitcast_fusion.9
  29.2 1.3 multiply_convert_fusion.6
  32.8 2.4 add_convert_fusion
  36.1 1.3 multiply_convert_fusion.8
  38.1 2.0 convolution_add_fusion
  41.0 13.0 %all-gather.2 = bf16[8,1,64]{2,1,0:T(2,128)(2,1)S(1)} all-gather(bf16[1,1,64]{2,1,0:T(2,128)(2,1)S(1)} %copy-done.21), channel_id=4, replica_groups=mesh['tm'=8,'batch'=4] {'tm'}, dimensions={0}, use_global_device_ids=true | all-gather | bytes 1152 | tf_op jit(solution)/shard_map/all_gather | solution.py:41
  54.9 7.8 %all-gather = f32[8,1,64]{2,1,0:T(1,128)S(1)} all-gather(f32[1,1,64]{2,1,0:T(1,128)S(1)} %get-tuple-element.350), channel_id=2, replica_groups=mesh['tm'=8,'batch'=4] {'tm'}, dimensions={0}, use_global_device_ids=true | all-gather | bytes 2304 | tf_op jit(solution)/shard_map/all_gather | solution.py:24
  63.1 31.3 %all-gather.9.cloned.1.call-done = bf16[512,64,64]{2,1,0:T(8,128)(2,1)} async-done(((bf16[64,64,64]{2,1,0:T(8,128)(2,1)}), bf16[512,64,64]{2,1,0:T(8,128)(2,1)}) %all-gather.9.cloned.1.call-update) | async-done | bytes 4194320 | tf_op jit(solution)/shard_map/all_gather | solution.py:41
  94.7 12.9 %while.18 = (s32[]{:T(128)}, f32[64,64,64]{2,1,0:T(8,128)S(1)}, s32[]{:T(128)}, bf16[8,64]{1,0:T(8,128)(2,1)S(1)}, bf16[8,64,64,64]{3,2,1,0:T(8,128)(2,1)}, /*index=5*/s32[]{:T(128)}, s32[]{:T(128)}, s32[]{:T(128)}, s32[]{:T(128)}) while((s32[]{:T(128)}, f32[64,64,64]{2,1,0:T(8,128)S(1)}, s32[]{:T(128)}, bf16[8,64]{1,0:T(8,128)(2,1)S(1)}, ...), condition=%wide.region_5.6_spmd, body=%wide.region_4.5_spmd.sunk | while | flops 786502 | bytes 2622235 | solution.py:56
  94.7 1.7 convert_add_fusion.2
  96.4 1.7 convert_add_fusion.2
  98.2 1.7 convert_add_fusion.2
  99.9 1.7 convert_add_fusion.2
  101.7 1.9 convert_add_fusion.2
  103.6 1.9 convert_add_fusion.2
  105.6 1.8 convert_add_fusion.2
  107.6 1.5 subtract_convert_fusion
  109.1 1.6 copy.106
  113.0 2.5 fusion.16
  115.5 1.3 copy.108
  116.8 12.6 %rev.16 = bf16[128,4096]{1,0:T(8,128)(2,1)S(1)} reverse(bf16[128,4096]{1,0:T(8,128)(2,1)} %copy.108), dimensions={0} | reverse | bytes 2097152 | tf_op jit(solution)/shard_map/rev | solution.py:192
  129.4 56.8 %all-gather.7.cloned.1.call-done = f32[512,64,64]{2,1,0:T(8,128)} async-done(((f32[64,64,64]{2,1,0:T(8,128)}), f32[512,64,64]{2,1,0:T(8,128)}) %all-gather.7.cloned.1.call-update) | async-done | bytes 8388624 | tf_op jit(solution)/shard_map/all_gather | solution.py:24
  186.2 14.8 %while.19 = (s32[]{:T(128)}, f32[64,64,64]{2,1,0:T(8,128)S(1)}, s32[]{:T(128)}, f32[8,64]{1,0:T(8,128)S(1)}, f32[8,64,64,64]{3,2,1,0:T(8,128)}, /*index=5*/s32[]{:T(128)}, s32[]{:T(128)}) while((s32[]{:T(128)}, f32[64,64,64]{2,1,0:T(8,128)S(1)}, s32[]{:T(128)}, f32[8,64]{1,0:T(8,128)S(1)}, f32[8,64,64,64]{3,2,1,0:T(8,128)}, ...), condition=%wide.region_2.3_spmd.clone, body=%wide.region_1.2_spmd.clone.sunk | while | flops 1048580 | bytes 3146609 | solution.py:33
  186.2 2.1 fusion.86
  188.3 2.1 fusion.86
  190.4 2.1 fusion.86
  192.6 2.1 fusion.86
  194.7 2.1 fusion.86
  196.8 2.1 fusion.86
  198.9 2.1 fusion.86
  201.0 1.9 subtract_convert_fusion.1
  202.9 1.6 copy.96
  204.6 1.8 fusion.67
  208.9 2.5 fusion.18
  211.4 1.6 bitcast_convert_fusion.1
  213.0 1.9 copy.109
  214.9 2.1 multiply_reduce_fusion
  217.3 2.8 copy.110
  220.7 22.4 %reduce = bf16[4096,128]{1,0:T(8,128)(2,1)S(1)} reduce(bf16[4096,1,128]{2,1,0:T(2,128)(2,1)S(1)} %bitcast.171, bf16[]{:T(256)} %broadcast.103), dimensions={1}, to_apply=%bitcast.145.reduce_sub_computation | reduce | bytes 2097154
  243.4 17.9 %all_to_all.30 = bf16[8,2,32768]{2,1,0:T(2,128)(2,1)S(1)} all-to-all(bf16[8,2,32768]{2,1,0:T(2,128)(2,1)S(1)} %reshape.251), channel_id=1, replica_groups=mesh['tm'=8,'batch'=4] {'tm'}, dimensions={0} | all-to-all | bytes 2097152 | tf_op jit(solution)/shard_map/all_to_all | solution.py:197
  262.5 1.3 copy.111
  263.8 2.8 copy.119
  266.6 7.0 %reduce.1 = bf16[1024,512]{1,0:T(8,128)(2,1)S(1)} reduce(bf16[1024,1,512]{2,1,0:T(2,128)(2,1)S(1)} %bitcast.172, bf16[]{:T(256)} %broadcast.103), dimensions={1}, to_apply=%bitcast.160.reduce_sub_computation | reduce | bytes 2097154
  274.5 29.5 %all_to_all.31 = bf16[4,2,65536]{2,1,0:T(2,128)(2,1)S(1)} all-to-all(bf16[4,2,65536]{2,1,0:T(2,128)(2,1)S(1)} %reshape.253), channel_id=1, replica_groups=mesh['tm'=8,'batch'=4] {'batch'}, dimensions={0} | all-to-all | bytes 2097152 | tf_op jit(solution)/shard_map/all_to_all | solution.py:196
  (132 shorter events, 30.1 us)
Async XLA Ops:
  6.5 18.0 %copy-start.1 = (bf16[1,128,4096]{2,1,0:T(8,128)(2,1)S(1)}, bf16[1,128,4096]{2,1,0:T(8,128)(2,1)}, u32[]{:S(2)}) copy-start(bf16[1,128,4096]{2,1,0:T(8,128)(2,1)} %param.14) | copy-start | bytes 3145732
  6.5 87.9 %all-gather.9.cloned.1.call-start = ((), (), s32[]{:S(2)}) async-start(), calls=%async_computation.3 | async-start | bytes 9437184 | tf_op jit(solution)/shard_map/all_gather | solution.py:41
  8.2 19.1 %collective-permute-start = (bf16[3,4224]{1,0:T(4,128)(2,1)S(1)}, bf16[3,4224]{1,0:T(4,128)(2,1)S(1)}, u32[]{:S(2)}, u32[]{:S(2)}) collective-permute-start(bf16[3,4224]{1,0:T(4,128)(2,1)S(1)} %pad_maximum_fusion), channel_id=1, source_target_pairs={{0,4},{4,8},{8,12},{12,16},{16,20},{20,24},{24,28},{1,5},{5,9},{9,... | collective-permute-start | bytes 76040 | tf_op jit(solution)/shard_map/ppermute | solution.py:19
  11.3 15.2 %collective-permute-start.1 = (bf16[3,4224]{1,0:T(4,128)(2,1)S(1)}, bf16[3,4224]{1,0:T(4,128)(2,1)S(1)}, u32[]{:S(2)}, u32[]{:S(2)}) collective-permute-start(bf16[3,4224]{1,0:T(4,128)(2,1)S(1)} %pad_maximum_fusion.1), channel_id=1, source_target_pairs={{4,0},{8,4},{12,8},{16,12},{20,16},{24,20},{28,24},{5,1},{9,5},{13... | collective-permute-start | bytes 76040 | tf_op jit(solution)/shard_map/ppermute | solution.py:19
  27.3 1.9 copy-start.15
  30.6 0.8 copy-start.9
  30.6 0.8 copy-start.10
  31.3 3.9 %copy-start.6 = (bf16[128,4096]{0,1:T(8,128)(2,1)}, bf16[128,4096]{0,1:T(8,128)(2,1)S(1)}, u32[]{:S(2)}) copy-start(bf16[128,4096]{0,1:T(8,128)(2,1)S(1)} %copy.98) | copy-start | bytes 3145732
  31.5 4.0 %copy-start.8 = (bf16[1,128,128]{2,1,0:T(8,128)(2,1)S(1)}, bf16[1,128,128]{2,1,0:T(8,128)(2,1)}, u32[]{:S(2)}) copy-start(bf16[1,128,128]{2,1,0:T(8,128)(2,1)} %param.18) | copy-start | bytes 98308
  32.8 2.9 copy-start.16
  35.2 0.8 copy-start.11
  35.3 0.8 copy-start.12
  35.3 0.8 copy-start.13
  35.3 0.8 copy-start.14
  35.3 150.9 %all-gather.7.cloned.1.call-start = ((), (), s32[]{:S(2)}) async-start(), calls=%async_computation.2 | async-start | bytes 18874368 | tf_op jit(solution)/shard_map/all_gather | solution.py:24
  38.1 2.1 copy-start.2
  38.1 3.0 copy-start.21
  40.1 22.6 %copy-start.20 = (f32[2,64]{1,0:T(2,128)S(1)}, f32[2,64]{1,0:T(2,128)}, u32[]{:S(2)}) copy-start(f32[2,64]{1,0:T(2,128)} %param.22) | copy-start | bytes 1540
  111.8 1.2 copy-start.7
  111.8 1.2 copy-start.18
  115.5 70.7 %copy-start = (f32[64,64,64]{2,1,0:T(8,128)S(1)}, f32[64,64,64]{2,1,0:T(8,128)}, u32[]{:S(2)}) copy-start(f32[64,64,64]{2,1,0:T(8,128)} %custom-call) | copy-start | bytes 3145732
  204.5 1.8 copy-start.4
  206.3 1.1 copy-start.17
  207.0 1.2 copy-start.3
  207.0 1.9 copy-start.5
  214.9 2.1 copy-start.19
Sparse Core Ops, SparseCore 0:
  35.4 59.0 all-gather.8
  96.3 89.8 all-gather.6
where the time goes:
time: 316 us; the launch traced here: 313 us
  waiting for transfers between devices  88.1 us (28%)
  other arithmetic  70.9 us (22%)
  blocking collectives  68.3 us (22%)
  local copies, waits for them, and re-layouts  54.6 us (17%)
  between operations  14 us (4%)
  matrix products  12.8 us (4%)
  starting transfers between devices  3.7 us (1%)
    all_gather x1, waiting for transfers between devices, entering(): pieces = jax.tree.map(lambda part: lax.all_gather(part, axis), value)  56.8 us
    all_gather x1, waiting for transfers between devices, carried_in(): lax.all_gather(a.astype(kind), axis)  31.3 us
    all_to_all x1, blocking collectives, shards(): lax.all_to_all(lax.all_to_all(normed[None], 'tm', split_axis=2, concat_ax...  29.5 us
    unnamed x3, other arithmetic  29.4 us
    all_to_all x1, blocking collectives, shards(): lax.all_to_all(normed[None], 'tm', split_axis=2, concat_axis=1, tiled=True)  17.9 us
    select_n x7, other arithmetic, lap(): jnp.where(position < mine, new, old)  14.5 us
    all_gather x1, blocking collectives, carried_in(): lax.all_gather(a.astype(kind), axis)  13 us
    rev x1, local copies, waits for them, and re-layouts, shards(): backward_out = block_outputs(bwd_parts, bwd_in[1], skip_gain[1])[::-1]  12.6 us
  transfers between devices with their start and end apart: 4, of which 2 were waited for; matrix products, arithmetic and copies ran while one was open for 18% of the time, Pallas kernels for 0%

commit v1 on v0

v1 whole, which is shorter than its diff:
```python
import functools

import jax
import jax.numpy as jnp
from jax import lax
from jax.experimental import pallas as pl
from jax.experimental.pallas import tpu as pltpu
from jax.sharding import PartitionSpec as P

INNER = 4096
HEADDIM = 64
STATE = 64
HEADS = 64
ROWS = 128
RIM = 16
EPSILON = 1e-05
LOG2E = 1.4426950408889634
MASKED = -1e30

F32 = jnp.float32
BF16 = jnp.bfloat16


def dot(a, b, **kwargs):
    return jnp.dot(a, b, preferred_element_type=F32, **kwargs)


def split_bf16(value):
    high = value.astype(BF16)
    low = (value - high.astype(F32)).astype(BF16)
    return jnp.concatenate([high, low], axis=1)


def half_silu(half):
    return half + half * jnp.tanh(half)


def mixer_kernel(
    tm_count,
    batch_count,
    sig_ref,
    gate_ref,
    bcf_ref,
    bcb_ref,
    step_ref,
    rate_ref,
    cw_ref,
    cb_ref,
    skip_ref,
    gain_ref,
    out_ref,
    hl_sig,
    hr_sig,
    hl_bc,
    hr_bc,
    tot_buf,
    ext,
    ext_bc,
    xs,
    rt,
    roll_a,
    we_f,
    we_dw,
    keep,
    snd,
    pin,
    csnd,
    crecv,
    esnd,
    ein,
    eown,
    yloc,
    outs,
    landing,
    inv_snd,
    inv_buf,
    halo_ssem,
    halo_rsem,
    tot_ssem,
    tot_rsem,
    pin_ssem,
    pin_rsem,
    chip_ssem,
    chip_rsem,
    ein_ssem,
    ein_rsem,
    out_ssem,
    out_rsem,
    inv_ssem,
    inv_rsem,
):
    T = tm_count
    M = T // 2
    CW = INNER // T
    HG = CW // HEADDIM
    per = T // batch_count
    me = lax.axis_index("tm")
    rec = lax.axis_index("batch")
    core = lax.rem(me, 2)
    chip = me // 2
    forward = core == 1
    partner = me + 1 - 2 * core
    dest = me // per
    place = jnp.where(forward, chip, M - 1 - chip)

    def at(tm, batch=None):
        return {"tm": tm, "batch": rec if batch is None else batch}

    barrier = pltpu.get_barrier_semaphore()

    def greet(tm, batch):
        pl.semaphore_signal(
            barrier, inc=1, device_id={"tm": tm, "batch": batch},
            device_id_type=pl.DeviceIdType.MESH,
        )

    own_dest = dest == rec
    for j in range(T):

        @pl.when(j != me)
        def _():
            greet(j, rec)

        @pl.when(jnp.logical_or(j != me, jnp.logical_not(own_dest)))
        def _():
            greet(j, dest)

    for b in range(batch_count):
        for q in range(per):

            @pl.when(jnp.logical_or(b != rec, rec * per + q != me))
            def _():
                greet(rec * per + q, b)

    pl.semaphore_wait(barrier, (T - 1) + 2 * (T - jnp.where(own_dest, 1, 0)))

    def remote(src, dst, ssem, rsem, device):
        return pltpu.make_async_remote_copy(
            src_ref=src, dst_ref=dst, send_sem=ssem, recv_sem=rsem,
            device_id=device, device_id_type=pl.DeviceIdType.MESH,
        )

    to_right = [
        remote(sig_ref.at[pl.ds(ROWS - RIM, RIM)], hl_sig, halo_ssem.at[0], halo_rsem.at[0], at(me + 1)),
        remote(bcf_ref.at[pl.ds(ROWS - RIM, RIM)], hl_bc, halo_ssem.at[1], halo_rsem.at[1], at(me + 1)),
    ]
    to_left = [
        remote(sig_ref.at[pl.ds(0, RIM)], hr_sig, halo_ssem.at[2], halo_rsem.at[2], at(me - 1)),
        remote(bcb_ref.at[pl.ds(0, RIM)], hr_bc, halo_ssem.at[3], halo_rsem.at[3], at(me - 1)),
    ]

    @pl.when(me < T - 1)
    def _():
        for copy in to_right[::-1]:
            copy.start()

    @pl.when(me > 0)
    def _():
        for copy in to_left[::-1]:
            copy.start()

    raw = step_ref[...].astype(F32)
    step = jnp.maximum(raw, 0.0) + jnp.log1p(jnp.exp(-jnp.abs(raw)))
    rate = jnp.concatenate([rate_ref[0:1, :], rate_ref[1:2, :]], axis=1)
    log_decay = -step * rate
    row = lax.broadcasted_iota(jnp.int32, (ROWS, ROWS), 0)
    col = lax.broadcasted_iota(jnp.int32, (ROWS, ROWS), 1)
    lower = row >= col
    upper = row <= col
    fwd_lane = col < HEADS
    high = lax.Precision.HIGHEST
    cum = jnp.where(
        fwd_lane,
        dot(lower.astype(F32), log_decay, precision=high),
        dot(upper.astype(F32), log_decay, precision=high),
    )
    total = jnp.where(fwd_lane[0:1], cum[ROWS - 1 : ROWS], cum[0:1])
    tot_buf[me] = jnp.broadcast_to(total, (8, ROWS))

    def tot_copy(j):
        return remote(tot_buf.at[me], tot_buf.at[me], tot_ssem.at[j], tot_rsem.at[me], at(j))

    for j in range(T):

        @pl.when(j != me)
        def _():
            tot_copy(j).start()

    we_f[0:ROWS] = split_bf16(jnp.exp(total - cum) * step)
    we_f[ROWS : 2 * ROWS] = split_bf16(jnp.exp(cum))
    rt[...] = (LOG2E * (jnp.log(step) - cum)).T
    scaled_cum = LOG2E * cum
    roll_a[...] = scaled_cum
    skip = jnp.concatenate([skip_ref[0:1, :], skip_ref[1:2, :]], axis=1)
    skip_split = split_bf16(jnp.broadcast_to(skip, (16, 2 * HEADS)))
    own_dir = (lax.broadcasted_iota(jnp.int32, (1, 2 * HEADS), 1) < HEADS) == forward

    def spread(g, first):
        k = lax.broadcasted_iota(jnp.int32, (4 * HEADS, CW), 0)
        c = lax.broadcasted_iota(jnp.int32, (4 * HEADS, CW), 1)
        head = first + g * HG + c // HEADDIM
        return (lax.rem(k, 2 * HEADS) == head).astype(F32).astype(BF16)

    @pl.when(me == 0)
    def _():
        hl_sig[...] = jnp.zeros_like(hl_sig)
        hl_bc[...] = jnp.zeros_like(hl_bc)

    @pl.when(me == T - 1)
    def _():
        hr_sig[...] = jnp.zeros_like(hr_sig)
        hr_bc[...] = jnp.zeros_like(hr_bc)

    @pl.when(me > 0)
    def _():
        for copy in to_right:
            copy.wait_recv()

    @pl.when(me < T - 1)
    def _():
        for copy in to_left:
            copy.wait_recv()

    def conv(buf, direction, cols):
        half = 0.5 * cb_ref[direction : direction + 1, cols]
        for k in range(4):
            start = 5 + k if direction == 0 else 11 - k
            tap = 0.5 * cw_ref[direction, k : k + 1, cols]
            half = half + tap * buf[start : start + ROWS, :]
        return half_silu(half).astype(BF16)

    bc_cols = slice(INNER, INNER + 2 * STATE)
    ext_bc[0:8] = hl_bc[...].astype(F32)[8:16]
    ext_bc[8 : 8 + ROWS] = bcf_ref[...].astype(F32)
    bc_f = conv(ext_bc, 0, bc_cols)
    ext_bc[8 : 8 + ROWS] = bcb_ref[...].astype(F32)
    ext_bc[8 + ROWS : 16 + ROWS] = hr_bc[...].astype(F32)[0:8]
    bc_b = conv(ext_bc, 1, bc_cols)
    bt_f = bc_f.astype(F32).T[:STATE].astype(BF16)
    bt_b = bc_b.astype(F32).T[:STATE].astype(BF16)
    c_f = bc_f[:, STATE:]
    c_b = bc_b[:, STATE:]
    scores_f = dot(c_f, bt_f)
    scores_b = dot(c_b, bt_b)
    bias_f = jnp.where(lower, 0.0, MASKED)
    bias_b = jnp.where(upper, 0.0, MASKED)

    def cols_of(g):
        return pl.ds(pl.multiple_of(g * CW, CW), CW)

    def pin_copy(g):
        return remote(snd.at[g], pin.at[g], pin_ssem.at[g], pin_rsem.at[g], at(partner))

    def chip_copy(g, target):
        tm = jnp.where(forward, 2 * target + 1, 2 * (M - 1 - target))
        return remote(
            csnd.at[g], crecv.at[place, g], chip_ssem.at[target, g], chip_rsem.at[place, g], at(tm)
        )

    def recv_chip(g, source):
        return remote(
            csnd.at[g], crecv.at[source, g], chip_ssem.at[source, g], chip_rsem.at[source, g], at(partner)
        )

    own_first = jnp.where(forward, 0, HEADS)

    def combine(g):
        pin_copy(g).wait_recv()
        factor = jnp.where(
            forward,
            dot(we_f[2 * ROWS - 16 :], spread(g, 0))[15:16],
            dot(we_f[ROWS : ROWS + 16], spread(g, HEADS))[0:1],
        )
        csnd[g] = (pin[g].astype(F32) * factor + keep[g]).astype(BF16)
        for target in range(1, M):

            @pl.when(place < target)
            def _():
                chip_copy(g, target).start()

    def first(g, _):
        cols = cols_of(g)
        ext[0:8] = hl_sig[:, cols].astype(F32)[8:16]
        ext[8 : 8 + ROWS] = sig_ref[:, cols].astype(F32)
        ext[8 + ROWS : 16 + ROWS] = hr_sig[:, cols].astype(F32)[0:8]
        x_f = conv(ext, 0, cols)
        x_b = conv(ext, 1, cols)
        xs[0:ROWS, cols] = x_f
        xs[ROWS : 2 * ROWS, cols] = x_b
        w_f = dot(we_f[0:ROWS], spread(g, 0))
        w_b = dot(we_f[0:ROWS], spread(g, HEADS))
        state_f = dot(bt_f, (x_f.astype(F32) * w_f).astype(BF16))
        state_b = dot(bt_b, (x_b.astype(F32) * w_b).astype(BF16))
        snd[g] = jnp.where(forward, state_b, state_f).astype(BF16)
        keep[g] = jnp.where(forward, state_f, state_b)
        pin_copy(g).start()

        @pl.when(g > 0)
        def _():
            combine(g - 1)

        return 0

    lax.fori_loop(0, T, first, 0)
    combine(T - 1)

    lane = lax.broadcasted_iota(jnp.int32, (ROWS, 2 * HEADDIM), 1)

    def local(g, _):
        rolled = pltpu.roll(roll_a[...], lax.rem(2 * HEADS - g * HG, 2 * HEADS), 1)
        skips_f = dot(skip_split, spread(g, 0))[0:1]
        skips_b = dot(skip_split, spread(g, HEADS))[0:1]

        def mixing(h):
            a_f = rolled[:, h : h + 1]
            a_b = rolled[:, HEADS + h : HEADS + h + 1]
            r_f = rt[pl.ds(g * HG + h, 1), :]
            r_b = rt[pl.ds(HEADS + g * HG + h, 1), :]
            mix_f = (scores_f * jnp.exp2((a_f + r_f) + bias_f)).astype(BF16)
            mix_b = (scores_b * jnp.exp2((a_b + r_b) + bias_b)).astype(BF16)
            return jnp.concatenate([mix_f, mix_b], axis=1)

        for pair in range(HG // 2):
            width = 2 * HEADDIM
            cols = pl.ds(pl.multiple_of(g * CW + pair * width, width), width)
            x_pair = xs[:, cols]
            stacked = jnp.concatenate([mixing(2 * pair), mixing(2 * pair + 1)], axis=0)
            both = dot(stacked, x_pair)
            out = jnp.where(lane < HEADDIM, both[:ROWS], both[ROWS:])
            inside = slice(pair * width, (pair + 1) * width)
            out = out + skips_f[:, inside] * x_pair[:ROWS].astype(F32)
            out = out + skips_b[:, inside] * x_pair[ROWS:].astype(F32)
            yloc[:, cols] = out
        return 0

    lax.fori_loop(0, T, local, 0)

    for j in range(T):

        @pl.when(j != me)
        def _():
            remote(tot_buf.at[j], tot_buf.at[j], tot_ssem.at[j], tot_rsem.at[j], at(partner)).wait_recv()

    rows = [tot_buf[partner][0:1]]
    chips = [tot_buf[2 * q][0:1] + tot_buf[2 * q + 1][0:1] for q in range(M)]
    for source in range(M - 1):
        sum_f = jnp.zeros((1, 2 * HEADS), F32)
        sum_b = jnp.zeros((1, 2 * HEADS), F32)
        for q in range(source + 1, M):
            sum_f = sum_f + jnp.where(q < place, chips[q], 0.0)
            sum_b = sum_b + jnp.where(q < place, chips[M - 1 - q], 0.0)
        rows.append(jnp.where(forward, sum_f, sum_b))
    padding = -len(rows) % 16
    rows = jnp.exp(jnp.concatenate(rows + [jnp.zeros((padding, 2 * HEADS), F32)], axis=0))
    we_dw[...] = split_bf16(jnp.where(own_dir, rows, 0.0))

    def ein_copy(g):
        return remote(esnd.at[g], ein.at[g], ein_ssem.at[g], ein_rsem.at[g], at(partner))

    def enter(s, _):
        g = lax.rem(me + s, T)
        factors = dot(we_dw[...], spread(g, own_first))
        esnd[g] = jnp.zeros((STATE, CW), BF16)
        entering = keep.at[g]
        entering[...] = jnp.zeros((STATE, CW), F32)
        for source in range(M - 1):

            @pl.when(source < place)
            def _():
                recv_chip(g, source).wait_recv()
                entering[...] += factors[source + 1 : source + 2] * crecv[source, g].astype(F32)

        value = entering[...]
        esnd[g] = value.astype(BF16)
        ein_copy(g).start()
        eown[g] = (value * factors[0:1] + pin[g].astype(F32)).astype(BF16)
        return 0

    lax.fori_loop(0, T, enter, 0)

    slot = lax.rem(me, per)

    def out_copy(g):
        return remote(
            outs.at[g], landing.at[rec * per + slot], out_ssem.at[g], out_rsem.at[rec * per + slot],
            at(g, dest),
        )

    def last(s, squares):
        g = lax.rem(partner + s, T)
        cols = cols_of(g)
        ein_copy(g).wait_recv()
        own, other = eown[g], ein[g]
        enter_f = jnp.where(forward, own, other)
        enter_b = jnp.where(forward, other, own)
        decay_f = dot(we_f[ROWS : 2 * ROWS], spread(g, 0))
        decay_b = dot(we_f[ROWS : 2 * ROWS], spread(g, HEADS))
        y = yloc[:, cols] + decay_f * dot(c_f, enter_f) + decay_b * dot(c_b, enter_b)
        gated = y * half_silu(0.5 * gate_ref[:, cols].astype(F32))
        for part in range(CW // 128):
            piece = gated[:, part * 128 : (part + 1) * 128]
            squares = squares + piece * piece
        outs[g] = gated.astype(BF16)
        mine = jnp.logical_and(own_dest, g == me)

        @pl.when(mine)
        def _():
            landing[rec * per + slot] = outs[g]

        @pl.when(jnp.logical_not(mine))
        def _():
            out_copy(g).start()

        return squares

    squares = lax.fori_loop(0, T, last, jnp.zeros((ROWS, 128), F32))
    mean = jnp.sum(squares.T, axis=0, keepdims=True) * (1.0 / INNER)
    inv_snd[...] = jnp.broadcast_to(lax.rsqrt(mean + EPSILON), (8, ROWS))

    def inv_copy(j):
        return remote(
            inv_snd, inv_buf.at[rec * per + slot], inv_ssem.at[j], inv_rsem.at[rec * per + slot],
            at(j, dest),
        )

    for j in range(T):
        mine = jnp.logical_and(own_dest, j == me)

        @pl.when(mine)
        def _():
            inv_buf[rec * per + slot] = inv_snd[...]

        @pl.when(jnp.logical_not(mine))
        def _():
            inv_copy(j).start()

    gain = gain_ref[:, cols_of(me)]

    for b in range(batch_count):
        for q in range(per):
            n = b * per + q
            mine = jnp.logical_and(b == rec, rec * per + q == me)

            @pl.when(jnp.logical_not(mine))
            def _():
                remote(outs.at[0], landing.at[n], out_ssem.at[0], out_rsem.at[n], at(partner)).wait_recv()
                remote(inv_snd, inv_buf.at[n], inv_ssem.at[0], inv_rsem.at[n], at(partner)).wait_recv()

            scale = jnp.broadcast_to(inv_buf[n][0:1], (ROWS, ROWS)).T
            for part in range(CW // 128):
                inside = slice(part * 128, (part + 1) * 128)
                piece = landing[n, :, inside].astype(F32) * scale * gain[:, inside]
                out_ref[b, q * ROWS : (q + 1) * ROWS, inside] = piece.astype(BF16)

    @pl.when(me < T - 1)
    def _():
        for copy in to_right:
            copy.wait_send()

    @pl.when(me > 0)
    def _():
        for copy in to_left:
            copy.wait_send()

    for j in range(T):

        @pl.when(j != me)
        def _():
            tot_copy(j).wait_send()

        @pl.when(jnp.logical_not(jnp.logical_and(own_dest, j == me)))
        def _():
            inv_copy(j).wait_send()
            out_copy(j).wait_send()

    def sent(g, _):
        pin_copy(g).wait_send()
        ein_copy(g).wait_send()
        for target in range(1, M):

            @pl.when(place < target)
            def _():
                chip_copy(g, target).wait_send()

        return 0

    lax.fori_loop(0, T, sent, 0)


def shards(tm_count, batch_count, signal, gate_input, bc_forward, bc_backward, step_raw,
           decay_rate, conv_weight, conv_bias, skip_gain, norm_gain):
    T, M = tm_count, tm_count // 2
    CW = INNER // T
    per = T // batch_count
    vmem = pltpu.VMEM
    dma = pltpu.SemaphoreType.DMA
    scratch = [
        vmem((RIM, INNER), BF16),
        vmem((RIM, INNER), BF16),
        vmem((RIM, 2 * STATE), BF16),
        vmem((RIM, 2 * STATE), BF16),
        vmem((T, 8, ROWS), F32),
        vmem((ROWS + 16, CW), F32),
        vmem((ROWS + 16, 2 * STATE), F32),
        vmem((2 * ROWS, INNER), BF16),
        vmem((2 * HEADS, ROWS), F32),
        vmem((ROWS, 2 * HEADS), F32),
        vmem((2 * ROWS, 4 * HEADS), BF16),
        vmem((-(-M // 16) * 16, 4 * HEADS), BF16),
        vmem((T, STATE, CW), F32),
        vmem((T, STATE, CW), BF16),
        vmem((T, STATE, CW), BF16),
        vmem((T, STATE, CW), BF16),
        vmem((M, T, STATE, CW), BF16),
        vmem((T, STATE, CW), BF16),
        vmem((T, STATE, CW), BF16),
        vmem((T, STATE, CW), BF16),
        vmem((ROWS, INNER), F32),
        vmem((T, ROWS, CW), BF16),
        vmem((T, ROWS, CW), BF16),
        vmem((8, ROWS), F32),
        vmem((T, 8, ROWS), F32),
        dma((4,)),
        dma((4,)),
        dma((T,)),
        dma((T,)),
        dma((T,)),
        dma((T,)),
        dma((M, T)),
        dma((M, T)),
        dma((T,)),
        dma((T,)),
        dma((T,)),
        dma((T,)),
        dma((T,)),
        dma((T,)),
    ]
    return pl.pallas_call(
        functools.partial(mixer_kernel, T, batch_count),
        out_shape=jax.ShapeDtypeStruct((batch_count, per * ROWS, CW), BF16),
        in_specs=[pl.BlockSpec(memory_space=pltpu.VMEM)] * 10,
        out_specs=pl.BlockSpec(memory_space=pltpu.VMEM),
        scratch_shapes=scratch,
        compiler_params=pltpu.CompilerParams(
            collective_id=0, has_side_effects=True, vmem_limit_bytes=48 * 2**20
        ),
        cost_estimate=pl.CostEstimate(
            flops=10**9, bytes_accessed=8 * 2**20, transcendentals=4 * 10**6
        ),
    )(signal[0], gate_input[0], bc_forward[0], bc_backward[0], step_raw[0],
      decay_rate, conv_weight, conv_bias, skip_gain, norm_gain.reshape(1, INNER))


def solution(mesh):
    in_specs = (P("batch", "tm", None),) * 5 + (P(),) * 5
    return jax.shard_map(
        functools.partial(shards, mesh.shape["tm"], mesh.shape["batch"]),
        mesh=mesh, in_specs=in_specs, out_specs=P(None, "batch", "tm"), check_vma=False,
    )
```

time: 316 us -> 110 us (0.35)
  Pallas kernels: 0 us -> 100 us
  waiting for transfers between devices: 88.1 us -> 0 us
  other arithmetic: 70.9 us -> 0 us
  blocking collectives: 68.3 us -> 0 us
  local copies, waits for them, and re-layouts: 54.6 us -> 8.77 us
  between operations: 14 us -> 0.02 us
  matrix products: 12.8 us -> 0 us
  starting transfers between devices: 3.7 us -> 0 us
    pallas_call x0 -> x1, Pallas kernels: none -> 100 us  [shards(): pl.pallas_call(functools.partial(mixer_kernel, T, batch_count), out_shape...]
    all_gather x2 -> x0, waiting for transfers between devices: 88.1 us -> none  [the longest x1 56.8 us: entering(): pieces = jax.tree.map(lambda part: lax.all_gather(part, axis), value)]
    all_to_all x2 -> x0, blocking collectives: 47.4 us -> none  [the longest x1 29.5 us: shards(): lax.all_to_all(lax.all_to_all(normed[None], 'tm', split_axis=2, concat_ax...]
    unnamed x3 -> x0, other arithmetic: 29.4 us -> none
    all_gather x2 -> x0, blocking collectives: 20.8 us -> none  [the longest x1 13 us: carried_in(): lax.all_gather(a.astype(kind), axis)]
    select_n x7 -> x0, other arithmetic: 14.5 us -> none  [lap(): jnp.where(position < mine, new, old)]
    rev x4 -> x0, local copies, waits for them, and re-layouts: 13.9 us -> none  [the longest x1 12.6 us: shards(): backward_out = block_outputs(bwd_parts, bwd_in[1], skip_gain[1])[::-1]]
    add x7 -> x0, other arithmetic: 12.4 us -> none  [combine(): earlier[1] * later[0][:, None, None] + later[1]]
  transfers between devices with their start and end apart: 4 -> 0, of which waited for: 2 -> 0; matrix products, arithmetic and copies ran while one was open for 18% -> 0% of each run, Pallas kernels for 0% -> 0%
where the time goes in v1:
time: 110 us; the launch traced here: 109 us
  Pallas kernels  100 us (91%)
  local copies, waits for them, and re-layouts  8.77 us (8%)
    pallas_call x1, Pallas kernels, shards(): pl.pallas_call(functools.partial(mixer_kernel, T, batch_count), out_shape...  100 us
    unnamed x21, local copies, waits for them, and re-layouts  8.77 us

profile of v1, /device:TPU:0, one launch (start us, length us, event | category | flops | bytes accessed | tf_op | source)
XLA Modules:
  0.0 109.0 jit_solution(18287315024536708999)
XLA Ops:
  0.0 0.0 copy-start.9
  0.0 0.0 copy-start.8
  0.0 0.7 copy-done.9
  0.7 0.0 copy-done.8
  0.7 0.0 copy-start
  0.7 1.2 %copy-done = bf16[1,128,4096]{2,1,0:T(8,128)(2,1)S(1)} copy-done((bf16[1,128,4096]{2,1,0:T(8,128)(2,1)S(1)}, bf16[1,128,4096]{2,1,0:T(8,128)(2,1)}, u32[]{:S(2)}) %copy-start) | copy-done | bytes 1048600
  1.9 0.0 copy-start.1
  1.9 1.2 %copy-done.1 = bf16[1,128,4096]{2,1,0:T(8,128)(2,1)S(1)} copy-done((bf16[1,128,4096]{2,1,0:T(8,128)(2,1)S(1)}, bf16[1,128,4096]{2,1,0:T(8,128)(2,1)}, u32[]{:S(2)}) %copy-start.1) | copy-done | bytes 1048600
  3.1 0.0 copy-start.2
  3.1 0.9 copy-done.2
  4.1 0.0 copy-start.3
  4.1 0.8 copy-done.3
  4.8 0.0 copy-start.4
  4.8 0.8 copy-done.4
  5.6 0.0 copy-start.5
  5.6 0.8 copy-done.5
  6.3 0.0 copy-start.6
  6.3 0.8 copy-done.6
  7.1 0.0 copy-start.7
  7.1 0.7 copy-done.7
  7.8 100.2 %shard_map.100 = bf16[4,256,512]{2,1,0:T(8,128)(2,1)S(1)} custom-call(bf16[128,4096]{1,0:T(8,128)(2,1)S(1)} %bitcast.6, bf16[128,4096]{1,0:T(8,128)(2,1)S(1)} %bitcast.7, bf16[128,128]{1,0:T(8,128)(2,1)S(1)} %bitcast.8, bf16[128,128]{1,0:T(8,128)(2,1)S(1)} %bitcast.9, bf16[128,128]{1,0:T(8,128)(2,1)S(1)} %bitcast.10, f32[2,64]{1,0:T(2,128)S(1)} %copy-done.8, ...), custom_call_target="tpu_custom_call" | custom-call | flops 1000000000 | bytes 8388608 | tf_op jit(solution)/shard_map/pallas_call | solution.py:538
  108.0 1.0 copy.12
Async XLA Ops:
  0.0 0.7 copy-start.9
  0.0 0.7 copy-start.8
  0.7 1.2 %copy-start = (bf16[1,128,4096]{2,1,0:T(8,128)(2,1)S(1)}, bf16[1,128,4096]{2,1,0:T(8,128)(2,1)}, u32[]{:S(2)}) copy-start(bf16[1,128,4096]{2,1,0:T(8,128)(2,1)} %param.10) | copy-start | bytes 3145732
  1.9 1.2 %copy-start.1 = (bf16[1,128,4096]{2,1,0:T(8,128)(2,1)S(1)}, bf16[1,128,4096]{2,1,0:T(8,128)(2,1)}, u32[]{:S(2)}) copy-start(bf16[1,128,4096]{2,1,0:T(8,128)(2,1)} %param.11) | copy-start | bytes 3145732
  3.1 0.9 copy-start.2
  4.1 0.8 copy-start.3
  4.8 0.8 copy-start.4
  5.6 0.8 copy-start.5
  6.3 0.8 copy-start.6
  7.1 0.7 copy-start.7

commit v2 on v1

--- a/solution.py
+++ b/solution.py
@@ -12,6 +12,7 @@
 STATE = 64
 HEADS = 64
 ROWS = 128
+LAG = 2
 RIM = 16
 EPSILON = 1e-05
 LOG2E = 1.4426950408889634
@@ -38,6 +39,17 @@
 def mixer_kernel(
     tm_count,
     batch_count,
+    sig_hbm,
+    gate_hbm,
+    bcf_hbm,
+    bcb_hbm,
+    step_hbm,
+    rate_hbm,
+    cw_hbm,
+    cb_hbm,
+    skip_hbm,
+    gain_hbm,
+    out_ref,
     sig_ref,
     gate_ref,
     bcf_ref,
@@ -48,7 +60,6 @@
     cb_ref,
     skip_ref,
     gain_ref,
-    out_ref,
     hl_sig,
     hr_sig,
     hl_bc,
@@ -71,6 +82,7 @@
     eown,
     yloc,
     outs,
+    mid,
     landing,
     inv_snd,
     inv_buf,
@@ -86,8 +98,11 @@
     ein_rsem,
     out_ssem,
     out_rsem,
+    fwd_ssem,
+    fwd_rsem,
     inv_ssem,
     inv_rsem,
+    load_sem,
 ):
     T = tm_count
     M = T // 2
@@ -106,6 +121,15 @@
     def at(tm, batch=None):
         return {"tm": tm, "batch": rec if batch is None else batch}
 
+    small = [(step_hbm, step_ref), (rate_hbm, rate_ref), (bcf_hbm, bcf_ref), (bcb_hbm, bcb_ref),
+             (skip_hbm, skip_ref), (cb_hbm, cb_ref), (cw_hbm, cw_ref), (sig_hbm, sig_ref)]
+    late = [(gate_hbm, gate_ref), (gain_hbm, gain_ref)]
+    loads = [
+        pltpu.make_async_copy(src, dst, load_sem.at[k]) for k, (src, dst) in enumerate(small + late)
+    ]
+    for load in loads:
+        load.start()
+
     barrier = pltpu.get_barrier_semaphore()
 
     def greet(tm, batch):
@@ -132,7 +156,13 @@
             def _():
                 greet(rec * per + q, b)
 
-    pl.semaphore_wait(barrier, (T - 1) + 2 * (T - jnp.where(own_dest, 1, 0)))
+    for b in range(batch_count):
+
+        @pl.when(b != rec)
+        def _():
+            greet(me, b)
+
+    pl.semaphore_wait(barrier, (T - 1) + 2 * (T - jnp.where(own_dest, 1, 0)) + batch_count - 1)
 
     def remote(src, dst, ssem, rsem, device):
         return pltpu.make_async_remote_copy(
@@ -141,12 +171,12 @@
         )
 
     to_right = [
-        remote(sig_ref.at[pl.ds(ROWS - RIM, RIM)], hl_sig, halo_ssem.at[0], halo_rsem.at[0], at(me + 1)),
-        remote(bcf_ref.at[pl.ds(ROWS - RIM, RIM)], hl_bc, halo_ssem.at[1], halo_rsem.at[1], at(me + 1)),
+        remote(sig_hbm.at[pl.ds(ROWS - RIM, RIM)], hl_sig, halo_ssem.at[0], halo_rsem.at[0], at(me + 1)),
+        remote(bcf_hbm.at[pl.ds(ROWS - RIM, RIM)], hl_bc, halo_ssem.at[1], halo_rsem.at[1], at(me + 1)),
     ]
     to_left = [
-        remote(sig_ref.at[pl.ds(0, RIM)], hr_sig, halo_ssem.at[2], halo_rsem.at[2], at(me - 1)),
-        remote(bcb_ref.at[pl.ds(0, RIM)], hr_bc, halo_ssem.at[3], halo_rsem.at[3], at(me - 1)),
+        remote(sig_hbm.at[pl.ds(0, RIM)], hr_sig, halo_ssem.at[2], halo_rsem.at[2], at(me - 1)),
+        remote(bcb_hbm.at[pl.ds(0, RIM)], hr_bc, halo_ssem.at[3], halo_rsem.at[3], at(me - 1)),
     ]
 
     @pl.when(me < T - 1)
@@ -159,6 +189,8 @@
         for copy in to_left[::-1]:
             copy.start()
 
+    for load in loads[: len(small)]:
+        load.wait()
     raw = step_ref[...].astype(F32)
     step = jnp.maximum(raw, 0.0) + jnp.log1p(jnp.exp(-jnp.abs(raw)))
     rate = jnp.concatenate([rate_ref[0:1, :], rate_ref[1:2, :]], axis=1)
@@ -381,10 +413,30 @@
     slot = lax.rem(me, per)
 
     def out_copy(g):
-        return remote(
-            outs.at[g], landing.at[rec * per + slot], out_ssem.at[g], out_rsem.at[rec * per + slot],
-            at(g, dest),
-        )
+        return remote(outs.at[g], mid.at[me], out_ssem.at[g], out_rsem.at[me], at(g))
+
+    def forward_copy(i):
+        n = rec * per + lax.rem(i, per)
+        return remote(mid.at[i], landing.at[n], fwd_ssem.at[i], fwd_rsem.at[n], at(me, i // per))
+
+    def pass_on(s):
+        there = lax.rem(me + T - s, T)
+        i = there + 1 - 2 * lax.rem(there, 2)
+
+        @pl.when(i != me)
+        def _():
+            remote(outs.at[i], mid.at[i], out_ssem.at[i], out_rsem.at[i], at(partner)).wait_recv()
+
+        @pl.when(i // per == rec)
+        def _():
+            landing[rec * per + lax.rem(i, per)] = mid[i]
+
+        @pl.when(i // per != rec)
+        def _():
+            forward_copy(i).start()
+
+    for load in loads[len(small) :]:
+        load.wait()
 
     def last(s, squares):
         g = lax.rem(partner + s, T)
@@ -401,15 +453,18 @@
             piece = gated[:, part * 128 : (part + 1) * 128]
             squares = squares + piece * piece
         outs[g] = gated.astype(BF16)
-        mine = jnp.logical_and(own_dest, g == me)
-
-        @pl.when(mine)
-        def _():
-            landing[rec * per + slot] = outs[g]
-
-        @pl.when(jnp.logical_not(mine))
+
+        @pl.when(g == me)
+        def _():
+            mid[me] = outs[g]
+
+        @pl.when(g != me)
         def _():
             out_copy(g).start()
+
+        @pl.when(s >= LAG)
+        def _():
+            pass_on(s - LAG)
 
         return squares
 
@@ -434,6 +489,9 @@
         def _():
             inv_copy(j).start()
 
+    for s in range(T - LAG, T):
+        pass_on(s)
+
     gain = gain_ref[:, cols_of(me)]
 
     for b in range(batch_count):
@@ -441,9 +499,12 @@
             n = b * per + q
             mine = jnp.logical_and(b == rec, rec * per + q == me)
 
+            @pl.when(b != rec)
+            def _():
+                remote(mid.at[0], landing.at[n], fwd_ssem.at[0], fwd_rsem.at[n], at(partner)).wait_recv()
+
             @pl.when(jnp.logical_not(mine))
             def _():
-                remote(outs.at[0], landing.at[n], out_ssem.at[0], out_rsem.at[n], at(partner)).wait_recv()
                 remote(inv_snd, inv_buf.at[n], inv_ssem.at[0], inv_rsem.at[n], at(partner)).wait_recv()
 
             scale = jnp.broadcast_to(inv_buf[n][0:1], (ROWS, ROWS)).T
@@ -471,7 +532,14 @@
         @pl.when(jnp.logical_not(jnp.logical_and(own_dest, j == me)))
         def _():
             inv_copy(j).wait_send()
+
+        @pl.when(j != me)
+        def _():
             out_copy(j).wait_send()
+
+        @pl.when(j // per != rec)
+        def _():
+            forward_copy(j).wait_send()
 
     def sent(g, _):
         pin_copy(g).wait_send()
@@ -494,7 +562,9 @@
     per = T // batch_count
     vmem = pltpu.VMEM
     dma = pltpu.SemaphoreType.DMA
-    scratch = [
+    args = (signal[0], gate_input[0], bc_forward[0], bc_backward[0], step_raw[0],
+            decay_rate, conv_weight, conv_bias, skip_gain, norm_gain.reshape(1, INNER))
+    scratch = [vmem(a.shape, a.dtype) for a in args] + [
         vmem((RIM, INNER), BF16),
         vmem((RIM, INNER), BF16),
         vmem((RIM, 2 * STATE), BF16),
@@ -518,6 +588,7 @@
         vmem((ROWS, INNER), F32),
         vmem((T, ROWS, CW), BF16),
         vmem((T, ROWS, CW), BF16),
+        vmem((T, ROWS, CW), BF16),
         vmem((8, ROWS), F32),
         vmem((T, 8, ROWS), F32),
         dma((4,)),
@@ -534,21 +605,23 @@
         dma((T,)),
         dma((T,)),
         dma((T,)),
+        dma((T,)),
+        dma((T,)),
+        dma((len(args),)),
     ]
     return pl.pallas_call(
         functools.partial(mixer_kernel, T, batch_count),
         out_shape=jax.ShapeDtypeStruct((batch_count, per * ROWS, CW), BF16),
-        in_specs=[pl.BlockSpec(memory_space=pltpu.VMEM)] * 10,
+        in_specs=[pl.BlockSpec(memory_space=pl.ANY)] * len(args),
         out_specs=pl.BlockSpec(memory_space=pltpu.VMEM),
         scratch_shapes=scratch,
         compiler_params=pltpu.CompilerParams(
-            collective_id=0, has_side_effects=True, vmem_limit_bytes=48 * 2**20
+            collective_id=0, has_side_effects=True, vmem_limit_bytes=60 * 2**20
         ),
         cost_estimate=pl.CostEstimate(
             flops=10**9, bytes_accessed=8 * 2**20, transcendentals=4 * 10**6
         ),
-    )(signal[0], gate_input[0], bc_forward[0], bc_backward[0], step_raw[0],
-      decay_rate, conv_weight, conv_bias, skip_gain, norm_gain.reshape(1, INNER))
+    )(*args)
 
 
 def solution(mesh):

time: 110 us -> 63.4 us (0.58)
  Pallas kernels: 100 us -> 61 us
  local copies, waits for them, and re-layouts: 8.77 us -> 2.26 us
    pallas_call x1, Pallas kernels: 100 us -> 61 us  [shards(): pl.pallas_call(functools.partial(mixer_kernel, T, batch_count), out_shape...]
    unnamed x21 -> x1, local copies, waits for them, and re-layouts: 8.77 us -> 2.26 us
where the time goes in v2:
time: 63.4 us; the launch traced here: 63.3 us
  Pallas kernels  61 us (96%)
  local copies, waits for them, and re-layouts  2.26 us (4%)
    pallas_call x1, Pallas kernels, shards(): pl.pallas_call(functools.partial(mixer_kernel, T, batch_count), out_shape...  61 us
    unnamed x1, local copies, waits for them, and re-layouts  2.26 us

profile of v2, /device:TPU:0, one launch (start us, length us, event | category | flops | bytes accessed | tf_op | source)
XLA Modules:
  0.0 63.3 jit_solution(16861192592724938245)
XLA Ops:
  0.0 61.0 %shard_map.100 = bf16[4,256,512]{2,1,0:T(8,128)(2,1)} custom-call(bf16[128,4096]{1,0:T(8,128)(2,1)} %bitcast.6, bf16[128,4096]{1,0:T(8,128)(2,1)} %bitcast.7, bf16[128,128]{1,0:T(8,128)(2,1)} %bitcast.8, bf16[128,128]{1,0:T(8,128)(2,1)} %bitcast.9, bf16[128,128]{1,0:T(8,128)(2,1)} %bitcast.10, f32[2,64]{1,0:T(2,128)} %rate_hbm.1, f32[2,4,4224]{2,1,0:T(4,128)} %cw_hbm.1, ...), custom_call_target="tpu_custom_call" | custom-call | flops 1000000000 | bytes 8388608 | tf_op jit(solution)/shard_map/pallas_call | solution.py:612
  61.0 2.3 %copy.12 = bf16[4,256,512]{2,1,0:T(8,128)(2,1)} copy(bf16[4,256,512]{2,1,0:T(8,128)(2,1)} %shard_map.100) | data formatting | bytes 2097152
